TPU v7x, 256 devices: a whole 4x4x8 slice. The times are simulated.
256 devices in a mesh: cell: 2 (over core), bini: 16 (over y, x), binj: 8 (over z).
Axes of the slice: x: 4, y: 4, z: 8, core: 2. Of those that a mesh axis runs over, the one named last changes fastest.
Arguments:
- contacts: float32 [32, 3072, 3072], P('cell', 'bini', 'binj'), may hold values from -49 to 49
- first_bins: float32 [24, 3072], P(None, ('bini', 'cell', 'binj')), may hold values from -24 to 24
- second_bins: float32 [24, 3072], P(None, ('binj', 'cell', 'bini')), may hold values from -24 to 24
Outputs:
- cell_factor: float32 [24, 32], P(None, 'cell')
- first_factor: float32 [24, 3072], P(None, ('bini', 'cell', 'binj'))
- second_factor: float32 [24, 3072], P(None, ('binj', 'cell', 'bini'))
All inputs are finite; a program needn't handle non-finite values.
Results may differ from a plain program's by a relative error of at most 0.0002.
Values sent between devices are 32-bit elements; how exact they have to be, the bound alone decides.
A program may use at most 64 MiB of HBM per device.

v0:
```python
import jax
import jax.numpy as jnp
from jax import lax
from jax.sharding import PartitionSpec as P

J = 3072
K = 3072
SWEEPS = 1


EPSILON = 1e-06
PRECISE = lax.Precision.HIGHEST


def gram_of(factor):
    return jnp.dot(factor, factor.T, precision=PRECISE, preferred_element_type=jnp.float32)


def normal_solve(system, right_terms):
    factor_low = jnp.linalg.cholesky(system)
    midway = lax.linalg.triangular_solve(factor_low, right_terms, left_side=True, lower=True)
    return lax.linalg.triangular_solve(
        factor_low, midway, left_side=True, lower=True, transpose_a=True
    )


def rescale(unscaled, unscaled_gram, row_total):
    column_scale = jnp.sqrt(jnp.diagonal(unscaled_gram) / row_total + EPSILON)
    return (
        unscaled / column_scale[:, None],
        unscaled_gram / (column_scale[:, None] * column_scale[None, :]),
    )


def total_gram(factor):
    return lax.psum(gram_of(factor), ("cell", "bini", "binj"))


def gather_first(factor):
    return lax.all_gather(factor, ("cell", "binj"), axis=1, tiled=True)


def gather_second(factor):
    return lax.all_gather(factor, ("cell", "bini"), axis=1, tiled=True)


def first_piece(first_block):
    width = first_block.shape[1] // lax.axis_size(("cell", "binj"))
    return lax.dynamic_slice_in_dim(first_block, lax.axis_index(("cell", "binj")) * width, width, 1)


def second_piece(second_block):
    width = second_block.shape[1] // lax.axis_size(("cell", "bini"))
    return lax.dynamic_slice_in_dim(
        second_block, lax.axis_index(("cell", "bini")) * width, width, 1
    )


def update_cells(cell_terms, system):
    cells_local = cell_terms.shape[1]
    cell_total = cells_local * lax.axis_size("cell")
    padded = jnp.zeros((cell_terms.shape[0], cell_total), jnp.float32)
    padded = lax.dynamic_update_slice_in_dim(
        padded, cell_terms, lax.axis_index("cell") * cells_local, 1
    )
    summed = lax.psum(padded, ("cell", "bini", "binj"))
    unscaled = normal_solve(system, summed)
    scaled, gram_cells = rescale(unscaled, gram_of(unscaled), cell_total)
    cells_now = lax.dynamic_slice_in_dim(
        scaled, lax.axis_index("cell") * cells_local, cells_local, 1
    )
    return (cells_now, gram_cells)


def update_first(first_terms, system):
    owned_terms = lax.psum_scatter(first_terms, ("cell", "binj"), scatter_dimension=1, tiled=True)
    unscaled = normal_solve(system, owned_terms)
    scaled, gram_first = rescale(unscaled, total_gram(unscaled), J)
    return (gather_first(scaled), gram_first)


def update_second(second_terms, system):
    owned_terms = lax.psum_scatter(second_terms, ("cell", "bini"), scatter_dimension=1, tiled=True)
    unscaled = normal_solve(system, owned_terms)
    scaled, gram_second = rescale(unscaled, total_gram(unscaled), K)
    return (gather_second(scaled), gram_second)


def per_device(contacts, first_bins, second_bins):
    cells_local = contacts.shape[0]
    first_block = gather_first(first_bins)
    second_block = gather_second(second_bins)
    gram_first = total_gram(first_bins)
    gram_second = total_gram(second_bins)

    def one_sweep(step_index, carried):
        cells_now, first_block, second_block, gram_first, gram_second = carried
        partial_first = lax.dot_general(
            second_block,
            contacts,
            (((1,), (2,)), ((), ())),
            precision=PRECISE,
            preferred_element_type=jnp.float32,
        )
        cell_terms = jnp.sum(partial_first * first_block[:, None, :], axis=2)
        cells_now, gram_cells = update_cells(cell_terms, gram_first * gram_second)
        first_terms = jnp.sum(partial_first * cells_now[:, :, None], axis=1)
        first_block, gram_first = update_first(first_terms, gram_cells * gram_second)
        partial_second = lax.dot_general(
            first_block,
            contacts,
            (((1,), (1,)), ((), ())),
            precision=PRECISE,
            preferred_element_type=jnp.float32,
        )
        second_terms = jnp.sum(partial_second * cells_now[:, :, None], axis=1)
        second_block, gram_second = update_second(second_terms, gram_cells * gram_first)
        return (cells_now, first_block, second_block, gram_first, gram_second)

    starting = (
        jnp.zeros((first_bins.shape[0], cells_local), jnp.float32),
        first_block,
        second_block,
        gram_first,
        gram_second,
    )
    cells_now, first_block, second_block, gram_first, gram_second = lax.fori_loop(
        0, SWEEPS, one_sweep, starting
    )
    return (cells_now, first_piece(first_block), second_piece(second_block))


def solution(mesh):
    placed = (
        P("cell", "bini", "binj"),
        P(None, ("bini", "cell", "binj")),
        P(None, ("binj", "cell", "bini")),
    )
    return jax.shard_map(
        per_device,
        mesh=mesh,
        in_specs=placed,
        out_specs=(
            P(None, "cell"),
            P(None, ("bini", "cell", "binj")),
            P(None, ("binj", "cell", "bini")),
        ),
        check_vma=False,
    )
```

profile of v0, /device:TPU:1, one launch (start us, length us, event | category | flops | bytes accessed | tf_op | source)
XLA Modules:
  0.0 627.9 jit_solution(9879103126594921531)
XLA Ops:
  0.7 69.1 %all-gather = f32[32,12,24]{2,1,0:T(8,128)S(1)} all-gather(f32[1,12,24]{2,1,0:T(8,128)} %bitcast.94), channel_id=1, replica_groups=mesh['cell'=2,'bini'=16,'binj'=8] {'cell','bini'}, dimensions={0}, use_global_device_ids=true | all-gather | bytes 38016 | tf_op jit(solution)/shard_map/all_gather | solution.py:44
  69.8 29.7 %all-gather.1 = f32[16,12,24]{2,1,0:T(8,128)S(1)} all-gather(f32[1,12,24]{2,1,0:T(8,128)} %bitcast.93), channel_id=1, replica_groups=mesh['cell'=2,'bini'=16,'binj'=8] {'cell','binj'}, dimensions={0}, use_global_device_ids=true | all-gather | bytes 19584 | tf_op jit(solution)/shard_map/all_gather | solution.py:40
  99.6 7.1 %multiply_reduce_fusion.1 = (f32[24,16]{0,1:T(8,128)S(1)}, f32[24,16,192]{2,0,1:T(8,128)S(1)}) fusion(f32[24,192]{1,0:T(8,128)S(1)} %bitcast.92, f32[16,192,384]{2,1,0:T(8,128)} %param.8, f32[384,24]{1,0:T(8,128)S(1)} %reshape.96), kind=kOutput, calls=%fused_computation.6 | convolution fusion | flops 339885696 | bytes 5070336 | tf_op jit(solution)/shard_map/while/body/eval_jaxpr/dot_general | solution.py:98
  107.1 73.2 %all-reduce.2 = (f32[24,32]{0,1:T(8,128)S(1)}, f32[24,24]{0,1:T(8,128)S(1)}, f32[24,24]{0,1:T(8,128)S(1)}) all-reduce(f32[24,32]{0,1:T(8,128)S(1)} %constant_dynamic-update-slice_fusion, f32[24,24]{0,1:T(8,128)S(1)} %fusion.28, f32[24,24]{0,1:T(8,128)S(1)} %fusion.29), channel_id=1, replica_groups=mesh['cell'=2,'bini'=16,'binj'=8] {'cell','bini','binj'}, use_global_device_ids=true, to_apply=%region_5.0 | all-reduce | flops 1920 | bytes 15360 | tf_op jit(solution)/shard_map/while/body/eval_jaxpr/psum | solution.py:66
  180.4 2.2 cholesky.59
  182.6 0.6 compare_reduce_fusion.2
  183.3 0.6 fusion.4
  183.9 1.8 custom-call.14
  186.4 0.8 gather_fusion
  187.4 2.2 cholesky.70
  190.2 0.6 fusion.5
  190.9 1.8 custom-call.24
  193.0 53.1 %all-reduce = f32[24,192]{1,0:T(8,128)S(1)} all-reduce(f32[24,192]{1,0:T(8,128)S(1)} %multiply_reduce_fusion), channel_id=2, replica_groups=mesh['cell'=2,'bini'=16,'binj'=8] {'cell','binj'}, use_global_device_ids=true, to_apply=%region_7.0.clone | all-reduce | flops 4608 | bytes 36864
  248.0 73.8 %psum.41 = f32[24,24]{0,1:T(8,128)S(1)} all-reduce(f32[24,24]{0,1:T(8,128)S(1)} %fusion.31), channel_id=1, replica_groups=mesh['cell'=2,'bini'=16,'binj'=8] {'cell','bini','binj'}, use_global_device_ids=true, to_apply=%region_8.12 | all-reduce | flops 576 | bytes 4608 | tf_op jit(solution)/shard_map/while/body/eval_jaxpr/psum | solution.py:36
  321.9 0.8 gather_fusion.1
  322.8 2.2 cholesky.81
  325.7 0.6 fusion.6
  326.3 1.8 custom-call.26
  328.2 28.8 %all-gather.2 = f32[16,12,24]{2,1,0:T(8,128)S(1)} all-gather(f32[1,12,24]{2,1,0:T(8,128)S(1)} %divide_bitcast_fusion.1), channel_id=1, replica_groups=mesh['cell'=2,'bini'=16,'binj'=8] {'cell','binj'}, dimensions={0}, use_global_device_ids=true | all-gather | bytes 19584 | tf_op jit(solution)/shard_map/while/body/eval_jaxpr/all_gather | solution.py:40
  357.0 4.7 fusion
  361.7 124.7 %all-reduce.1 = f32[24,384]{1,0:T(8,128)S(1)} all-reduce(f32[24,384]{1,0:T(8,128)S(1)} %fusion), channel_id=3, replica_groups=mesh['cell'=2,'bini'=16,'binj'=8] {'cell','bini'}, use_global_device_ids=true, to_apply=%region_10.14.clone | all-reduce | flops 9216 | bytes 73728
  488.2 73.3 %psum.42 = f32[24,24]{1,0:T(8,128)S(1)} all-reduce(f32[24,24]{1,0:T(8,128)S(1)} %fusion.32), channel_id=1, replica_groups=mesh['cell'=2,'bini'=16,'binj'=8] {'cell','bini','binj'}, use_global_device_ids=true, to_apply=%region_11.15 | all-reduce | flops 576 | bytes 4608 | tf_op jit(solution)/shard_map/while/body/eval_jaxpr/psum | solution.py:36
  561.6 0.8 gather_fusion.2
  562.4 64.3 %all-gather.3 = f32[32,12,24]{2,1,0:T(8,128)S(1)} all-gather(f32[1,12,24]{2,1,0:T(8,128)S(1)} %divide_bitcast_fusion), channel_id=1, replica_groups=mesh['cell'=2,'bini'=16,'binj'=8] {'cell','bini'}, dimensions={0}, use_global_device_ids=true | all-gather | bytes 38016 | tf_op jit(solution)/shard_map/while/body/eval_jaxpr/all_gather | solution.py:44
  (56 shorter events, 6.9 us)
Async XLA Ops:
  0.6 245.5 %copy-start.4 = (u32[256]{0:T(256)S(1)}, u32[256]{0:T(256)}, u32[]{:S(2)}) copy-start(u32[256]{0:T(256)} %constant.150) | copy-start | bytes 3076
  0.6 106.3 %copy-start.2 = (f32[24,12]{0,1:T(8,128)S(1)}, f32[24,12]{0,1:T(8,128)}, u32[]{:S(2)}) copy-start(f32[24,12]{0,1:T(8,128)} %param.10) | copy-start | bytes 3460
  0.7 106.1 %copy-start.1 = (f32[24,12]{0,1:T(8,128)S(1)}, f32[24,12]{0,1:T(8,128)}, u32[]{:S(2)}) copy-start(f32[24,12]{0,1:T(8,128)} %param.9) | copy-start | bytes 3460
  106.7 379.7 %copy-start.3 = (u32[256]{0:T(256)S(1)}, u32[256]{0:T(256)}, u32[]{:S(2)}) copy-start(u32[256]{0:T(256)} %constant.154) | copy-start | bytes 3076
  192.9 435.0 %copy-start = (f32[24,16]{0,1:T(8,128)}, f32[24,16]{0,1:T(8,128)S(1)}, u32[]{:S(2)}) copy-start(f32[24,16]{0,1:T(8,128)S(1)} %copy.45) | copy-start | bytes 4612
where the time goes:
time: 629 us; the launch traced here: 628 us
  blocking collectives  590 us (94%)
  other arithmetic  16.5 us (3%)
  matrix products  14 us (2%)
    unnamed x2, blocking collectives  178 us
    psum x2, blocking collectives, total_gram(): return lax.psum(gram_of(factor), ('cell', 'bini', 'binj'))  147 us
    all_gather x2, blocking collectives, gather_second(): return lax.all_gather(factor, ('cell', 'bini'), axis=1, tiled=True)  133 us
    psum x1, blocking collectives, update_cells(): summed = lax.psum(padded, ('cell', 'bini', 'binj'))  73.2 us
    all_gather x2, blocking collectives, gather_first(): return lax.all_gather(factor, ('cell', 'binj'), axis=1, tiled=True)  58.5 us

commit v1 on v0

v1 whole, which is shorter than its diff:
```python
import functools

import jax
import jax.numpy as jnp
from jax import lax
from jax.experimental import pallas as pl
from jax.experimental.pallas import tpu as pltpu
from jax.sharding import PartitionSpec as P

EPSILON = 1e-06
PRECISE = lax.Precision.HIGHEST
MESH = pl.DeviceIdType.MESH
R = 24
G = 3
SPREAD = 40
NT = (((1,), (1,)), ((), ()))


def lanes(shape):
    return lax.broadcasted_iota(jnp.int32, shape, 1)


def group(value, q):
    return value[8 * q : 8 * q + 8, :]


def stack(tiles):
    return jnp.concatenate(tiles, axis=0)


def turn(value, shift):
    if isinstance(shift, int):
        shift = shift % 128
        return value if shift == 0 else pltpu.roll(value, shift, 1)
    return pltpu.roll(value, shift, 1)


def pack(value, step, base=None):
    out = None
    for q in range(G):
        if base is None:
            tile = turn(group(value, q), step * q)
        else:
            tile = turn(group(value, q), lax.rem(base + step * q, 128))
        out = tile if out is None else out + tile
    return out


def unpack(tile, step, width, base=None):
    parts = []
    for q in range(G):
        if base is None:
            part = turn(tile, -step * q)
        else:
            part = turn(tile, lax.rem(256 - base - step * q, 128))
        parts.append(jnp.where(lanes(part.shape) < width, part, 0.0))
    return stack(parts)


def within(lane, start, width):
    return ((lane - start) & 127) < width


def spread(tile_at, count, width, tiles):
    lane = lanes((8, 128))
    out = [[jnp.zeros((8, 128), jnp.float32) for _ in range(tiles)] for _ in range(G)]
    for o in range(count):
        tile = tile_at(o)
        start = width * o
        for t in range(tiles):
            low, high = max(start, 128 * t), min(start + width, 128 * t + 128)
            if low >= high:
                continue
            for q in range(G):
                mask = within(lane, (low + SPREAD * q) % 128, high - low)
                out[q][t] = jnp.where(mask, tile, out[q][t])
    return [stack([turn(out[q][t], -SPREAD * q) for q in range(G)]) for t in range(tiles)]


def owner_tiles(tiles, count, width):
    lane = lanes((8, 128))
    moved = [[turn(group(tile, q), SPREAD * q) for tile in tiles] for q in range(G)]
    out = []
    for o in range(count):
        start = width * o
        packed = None
        for q in range(G):
            for t in range(len(tiles)):
                low, high = max(start, 128 * t), min(start + width, 128 * t + 128)
                if low >= high:
                    continue
                if packed is None:
                    packed = moved[q][t]
                else:
                    packed = jnp.where(within(lane, (low + SPREAD * q) % 128, high - low), moved[q][t], packed)
        out.append(packed)
    return out


def split(value):
    high = value.astype(jnp.bfloat16)
    return high, (value - high.astype(jnp.float32)).astype(jnp.bfloat16)


def split_rows(value):
    high = value.astype(jnp.bfloat16).astype(jnp.float32)
    return jnp.concatenate([high, value - high], axis=0).astype(jnp.bfloat16)


def gram(tiles):
    total = None
    for tile in tiles:
        tall = jnp.concatenate([tile, jnp.zeros((128 - R, 128), jnp.float32)], axis=0)
        part = lax.dot_general(tile, tall, NT, precision=PRECISE, preferred_element_type=jnp.float32)
        total = part if total is None else total + part
    return total


def inverse(a):
    lane, row = lanes((R, 128)), lax.broadcasted_iota(jnp.int32, (R, 128), 0)
    for k in range(R):
        pivot_row = a[k : k + 1, :]
        pivot_column = a[:, k : k + 1]
        over = 1.0 / a[k : k + 1, k : k + 1]
        new_row = jnp.where(lane[:1] == k, over, pivot_row * over)
        a = jnp.where(lane == k, 0.0, a) - pivot_column * new_row
        a = jnp.where(row == k, new_row, a)
    return a


def apply(matrix, value):
    total = None
    for s in range(R):
        term = matrix[:, s : s + 1] * value[s : s + 1, :]
        total = term if total is None else total + term
    return total


def diagonal_scales(raw, count):
    lane, row = lanes((R, 128)), lax.broadcasted_iota(jnp.int32, (R, 128), 0)
    diagonal = jnp.where(lane == row, raw, 0.0)
    column = jnp.sum(diagonal, axis=1, keepdims=True)
    across = jnp.sum(diagonal, axis=0, keepdims=True)
    return jnp.sqrt(column / count + EPSILON), jnp.sqrt(across / count + EPSILON)


def kernel(
    sizes,
    contacts,
    first_in,
    second_in,
    cell_out,
    first_out,
    second_out,
    x_full,
    x_high,
    x_low,
    first_land,
    second_land,
    first_pad,
    second_pad,
    first_slots,
    second_slots,
    terms_z,
    grams_xy,
    terms_xy,
    products,
    halves,
    half_in,
    halves_z,
    solved,
    raw_xy,
    owned_out,
    owned_in,
    norms_xy,
    norms_z,
    load_sem,
    send_sem,
    recv_sem,
):
    C, A, B, I, J, K = sizes
    cells, rows = x_full.shape[0], x_full.shape[1]
    width_first, width_second = rows // (C * B), x_full.shape[2] // (C * A)
    c, a, b = lax.axis_index("cell"), lax.axis_index("bini"), lax.axis_index("binj")
    in_cz, in_cxy = c * B + b, c * A + a
    other = (1 - c, a, b)
    lane8, lane24 = lanes((8, 128)), lanes((R, 128))

    loads = [
        pltpu.make_async_copy(second_in, second_land, load_sem.at[0]),
        pltpu.make_async_copy(first_in, first_land, load_sem.at[1]),
    ]
    for load in loads:
        load.start()

    def load_cell(i):
        return pltpu.make_async_copy(contacts.at[i], x_full.at[i], load_sem.at[2 + i])

    for i in range(cells):
        load_cell(i).start()

    barrier = pltpu.get_barrier_semaphore()

    def signal(device):
        pl.semaphore_signal(barrier, inc=1, device_id=device, device_id_type=MESH)

    def z_partner(k):
        return (c, a, lax.rem(b + k, B))

    def xy_partner(k):
        return (c, lax.rem(a + k, A), b)

    def cz_partner(k):
        return (lax.rem(c + k // B, C), a, lax.rem(b + lax.rem(k, B), B))

    def cxy_partner(k):
        return (lax.rem(c + k // A, C), lax.rem(a + lax.rem(k, A), A), b)

    def greet_cz(k, carry):
        signal(cz_partner(k))
        return carry

    def greet_cxy(k, carry):
        signal(cxy_partner(k))
        return carry

    lax.fori_loop(1, C * B, greet_cz, 0)
    lax.fori_loop(1, A, greet_cxy, 0)
    lax.fori_loop(A + 1, C * A, greet_cxy, 0)

    second_pad[...] = jnp.zeros_like(second_pad)
    first_pad[...] = jnp.zeros_like(first_pad)
    loads[0].wait()
    second_pad[:, :width_second] = second_land[...]
    loads[1].wait()
    first_pad[:, :width_first] = first_land[...]
    second_slots[in_cxy] = pack(second_pad[...], SPREAD, lax.rem(width_second * in_cxy, 128))
    first_slots[in_cz] = pack(first_pad[...], SPREAD, lax.rem(width_first * in_cz, 128))

    def send(source, target, number, device):
        pltpu.make_async_remote_copy(
            source, target, send_sem.at[number], recv_sem.at[number], device_id=device, device_id_type=MESH
        ).start()

    def send_all(source, target, number, partner, count):
        def one(k, carry):
            send(source, target, number, partner(k))
            return carry

        lax.fori_loop(1, count, one, 0)

    def arrived(like, number):
        pltpu.make_async_copy(like, like, recv_sem.at[number]).wait()

    def left(like, number):
        pltpu.make_async_copy(like, like, send_sem.at[number]).wait()

    def split_cell(i, carry):
        load_cell(i).wait()
        high, low = split(x_full[i])
        at = pl.ds(pl.multiple_of(i * rows, rows), rows)
        x_high[at, :] = high
        x_low[at, :] = low
        return carry

    lax.fori_loop(0, cells // 2, split_cell, 0)
    pl.semaphore_wait(barrier, C * B - 1 + C * (A - 1))

    mine = second_slots.at[in_cxy]
    send_all(mine, mine, 0, cxy_partner, C * A)
    mine = first_slots.at[in_cz]
    send_all(mine, mine, 1, cz_partner, C * B)
    lax.fori_loop(cells // 2, cells, split_cell, 0)

    arrived(second_slots.at[pl.ds(0, C * A - 1)], 0)
    second = spread(lambda o: second_slots[o], C * A, width_second, 3)
    second_rows = split_rows(jnp.concatenate(second, axis=1))
    arrived(first_slots.at[pl.ds(0, C * B - 1)], 1)
    first = spread(lambda o: first_slots[o], C * B, width_first, 2)
    first_turned = [turn(group(first[0], q), 64) for q in range(G)]
    first_turned = stack(first_turned)
    last_turned = stack([turn(group(first[1], q), 64) for q in range(G)])
    first_pair = [
        first[0],
        jnp.where(lane24 < 64, first[1], first_turned),
        jnp.where(lane24 < 64, first_turned, last_turned),
    ]

    cell_terms = jnp.zeros((R, 128), jnp.float32)
    for p in range(cells // 2):
        at = pl.ds(2 * rows * p, 2 * rows)
        big = lax.dot_general(second_rows, x_high[at, :], NT, preferred_element_type=jnp.float32)
        small = lax.dot_general(second_rows, x_low[at, :], NT, preferred_element_type=jnp.float32)
        both = (small[:R] + small[R:]) + big[R:] + big[:R]
        products[p] = both
        terms = [both[:, 128 * t : 128 * t + 128] * first_pair[t] for t in range(3)]
        even = jnp.sum(terms[0] + jnp.where(lane24 < 64, terms[1], 0.0), axis=1, keepdims=True)
        odd = jnp.sum(terms[2] + jnp.where(lane24 < 64, 0.0, terms[1]), axis=1, keepdims=True)
        cell_terms = jnp.where(lane24 == 2 * p, even, cell_terms)
        cell_terms = jnp.where(lane24 == 2 * p + 1, odd, cell_terms)

    terms_z[b] = pack(cell_terms, cells) + turn(pack(gram(second), R), 56)
    mine = terms_z.at[b]
    send_all(mine, mine, 2, z_partner, B)
    grams_xy[a] = pack(gram(first), R)
    mine = grams_xy.at[a]
    send_all(mine, mine, 3, xy_partner, A)

    arrived(terms_z.at[pl.ds(0, B - 1)], 2)
    summed = terms_z[0]
    for o in range(1, B):
        summed = summed + terms_z[o]
    terms_xy[in_cxy] = jnp.where(lane8 < G * cells, summed, 0.0)
    mine = terms_xy.at[in_cxy]
    send_all(mine, mine, 4, cxy_partner, C * A)

    gram_second = unpack(turn(summed, -56), R, R)
    arrived(grams_xy.at[pl.ds(0, A - 1)], 3)
    summed = grams_xy[0]
    for o in range(1, A):
        summed = summed + grams_xy[o]
    gram_first = unpack(summed, R, R)
    system = inverse(gram_first * gram_second)

    arrived(terms_xy.at[pl.ds(0, C * A - 1)], 4)
    cell_total = None
    for core in range(C):
        summed = terms_xy[core * A]
        for o in range(1, A):
            summed = summed + terms_xy[core * A + o]
        block = unpack(summed, cells, cells)
        block = stack([turn(group(block, q), cells * core) for q in range(G)])
        cell_total = block if cell_total is None else cell_total + block

    unscaled = apply(system, cell_total)
    scale = jnp.sqrt(jnp.sum(unscaled * unscaled, axis=1, keepdims=True) / I + EPSILON)
    cell_factor = unscaled / scale
    own_cells = stack([turn(group(cell_factor, q), lax.rem(128 - cells * c, 128)) for q in range(G)])
    cell_out[...] = own_cells[:, :cells]

    pair_sum = [jnp.zeros((R, 128), jnp.float32) for _ in range(3)]
    weights = []
    for p in range(cells // 2):
        even = jnp.broadcast_to(own_cells[:, 2 * p : 2 * p + 1], (R, 128))
        odd = jnp.broadcast_to(own_cells[:, 2 * p + 1 : 2 * p + 2], (R, 128))
        weight = [even, jnp.where(lane24 < 64, even, odd), odd]
        weights.append(weight)
        both = products[p]
        for t in range(3):
            pair_sum[t] = pair_sum[t] + both[:, 128 * t : 128 * t + 128] * weight[t]

    def half_turn(value):
        return stack([turn(group(value, q), 64) for q in range(G)])

    turned = [half_turn(pair_sum[1]), half_turn(pair_sum[2])]
    halves[0] = pair_sum[0] + jnp.where(lane24 < 64, turned[0], turned[1])
    halves[1] = jnp.where(lane24 < 64, pair_sum[1] + turned[1], 0.0)
    send(halves.at[1 - c], half_in, 5, other)

    raw = gram([unscaled])
    scale_column, scale_row = diagonal_scales(raw, I)
    gram_cells = jnp.where(lane24 < R, raw / (scale_column * scale_row), 0.0)

    arrived(half_in, 5)
    halves_z[b] = halves[c] + half_in[...]
    mine = halves_z.at[b]
    send_all(mine, mine, 6, z_partner, B)
    system = inverse(gram_cells * gram_second)
    arrived(halves_z.at[pl.ds(0, B - 1)], 6)
    summed = halves_z[0]
    for o in range(1, B):
        summed = summed + halves_z[o]
    solved[c] = apply(system, summed)
    mine = solved.at[c]
    send(mine, mine, 7, other)
    arrived(solved.at[0], 7)
    low, high = solved[0], solved[1]

    low_turned, high_turned = half_turn(low), half_turn(high)
    solved_pair = [
        low,
        jnp.where(lane24 < 64, high, low_turned),
        jnp.where(lane24 < 64, low_turned, high_turned),
    ]
    total = None
    for p in range(cells // 2):
        at = pl.ds(2 * rows * p, 2 * rows)
        left_rows = split_rows(
            jnp.concatenate([solved_pair[t] * weights[p][t] for t in range(3)], axis=1)
        )
        big = jnp.dot(left_rows, x_high[at, :], preferred_element_type=jnp.float32)
        small = jnp.dot(left_rows, x_low[at, :], preferred_element_type=jnp.float32)
        both = big + small
        total = both if total is None else total + both
    total = total[:R] + total[R:]

    tiles = owner_tiles([total[:, 128 * t : 128 * t + 128] for t in range(3)], C * A, width_second)
    for o in range(C * A):
        owned_out[o] = tiles[o]

    def send_owned(k, carry):
        goal = lax.rem(c + k // A, C) * A + lax.rem(a + lax.rem(k, A), A)
        send(owned_out.at[goal], owned_in.at[k - 1], 8, cxy_partner(k))
        return carry

    lax.fori_loop(1, C * A, send_owned, 0)

    raw_xy[a] = pack(gram([low, high]), R)
    mine = raw_xy.at[a]
    send_all(mine, mine, 9, xy_partner, A)
    arrived(raw_xy.at[pl.ds(0, A - 1)], 9)
    summed = raw_xy[0]
    for o in range(1, A):
        summed = summed + raw_xy[o]
    raw = unpack(summed, R, R)
    scale_column, scale_row = diagonal_scales(raw, J)
    gram_first = jnp.where(lane24 < R, raw / (scale_column * scale_row), 0.0)
    system = inverse(gram_cells * gram_first)
    start = width_first * in_cz
    at_low = lax.rem(256 - start, 128)
    piece = stack(
        [
            jnp.where(
                lane8 < 128 - start,
                turn(group(low, q), at_low),
                turn(group(high, q), at_low),
            )
            for q in range(G)
        ]
    )
    first_out[...] = (piece / scale_column)[:, :width_first]

    arrived(owned_in, 8)
    summed = owned_out[in_cxy]
    for o in range(C * A - 1):
        summed = summed + owned_in[o]
    second_terms = unpack(summed, SPREAD, width_second, lax.rem(width_second * in_cxy, 128))
    unscaled = apply(system, second_terms / scale_column)

    norm = jnp.sum(unscaled * unscaled, axis=1, keepdims=True)
    norm_tile = jnp.zeros((8, 128), jnp.float32)
    for q in range(G):
        norm_tile = jnp.where(lane8 == q, group(norm, q), norm_tile)
    norms_xy[in_cxy] = norm_tile
    mine = norms_xy.at[in_cxy]
    send_all(mine, mine, 10, cxy_partner, C * A)
    arrived(norms_xy.at[pl.ds(0, C * A - 1)], 10)
    summed = norms_xy[0]
    for o in range(1, C * A):
        summed = summed + norms_xy[o]
    norms_z[b] = summed
    mine = norms_z.at[b]
    send_all(mine, mine, 11, z_partner, B)
    arrived(norms_z.at[pl.ds(0, B - 1)], 11)
    summed = norms_z[0]
    for o in range(1, B):
        summed = summed + norms_z[o]
    norm = stack([summed[:, q : q + 1] for q in range(G)])
    second_out[...] = (unscaled / jnp.sqrt(norm / K + EPSILON))[:, :width_second]

    left(second_slots.at[pl.ds(0, C * A - 1)], 0)
    left(first_slots.at[pl.ds(0, C * B - 1)], 1)
    left(terms_z.at[pl.ds(0, B - 1)], 2)
    left(grams_xy.at[pl.ds(0, A - 1)], 3)
    left(terms_xy.at[pl.ds(0, C * A - 1)], 4)
    left(half_in, 5)
    left(halves_z.at[pl.ds(0, B - 1)], 6)
    left(solved.at[0], 7)
    left(owned_in, 8)
    left(raw_xy.at[pl.ds(0, A - 1)], 9)
    left(norms_xy.at[pl.ds(0, C * A - 1)], 10)
    left(norms_z.at[pl.ds(0, B - 1)], 11)


def per_device(sizes, contacts, first_bins, second_bins):
    C, A, B, I, J, K = sizes
    cells, rows, columns = contacts.shape
    f32 = jnp.float32

    def tiles(*lead):
        return pltpu.VMEM(lead + (8, 128), f32)

    return tuple(
        pl.pallas_call(
            functools.partial(kernel, sizes),
            out_shape=(
                jax.ShapeDtypeStruct((R, cells), f32),
                jax.ShapeDtypeStruct(first_bins.shape, f32),
                jax.ShapeDtypeStruct(second_bins.shape, f32),
            ),
            in_specs=[pl.BlockSpec(memory_space=pl.ANY)] * 3,
            out_specs=[pl.BlockSpec(memory_space=pltpu.VMEM)] * 3,
            scratch_shapes=[
                pltpu.VMEM((cells, rows, columns), f32),
                pltpu.VMEM((cells * rows, columns), jnp.bfloat16),
                pltpu.VMEM((cells * rows, columns), jnp.bfloat16),
                pltpu.VMEM(first_bins.shape, f32),
                pltpu.VMEM(second_bins.shape, f32),
                pltpu.VMEM((R, 128), f32),
                pltpu.VMEM((R, 128), f32),
                tiles(C * B),
                tiles(C * A),
                tiles(B),
                tiles(A),
                tiles(C * A),
                pltpu.VMEM((cells // 2, R, 2 * rows), f32),
                pltpu.VMEM((2, R, 128), f32),
                pltpu.VMEM((R, 128), f32),
                pltpu.VMEM((B, R, 128), f32),
                pltpu.VMEM((2, R, 128), f32),
                tiles(A),
                tiles(C * A),
                tiles(C * A - 1),
                tiles(C * A),
                tiles(B),
                pltpu.SemaphoreType.DMA((2 + cells,)),
                pltpu.SemaphoreType.DMA((12,)),
                pltpu.SemaphoreType.DMA((12,)),
            ],
            compiler_params=pltpu.CompilerParams(
                collective_id=0, has_side_effects=True, vmem_limit_bytes=40 * 1024 * 1024
            ),
            name="sweep",
        )(contacts, first_bins, second_bins)
    )


def solution(mesh):
    placed = (
        P("cell", "bini", "binj"),
        P(None, ("bini", "cell", "binj")),
        P(None, ("binj", "cell", "bini")),
    )

    def whole(contacts, first_bins, second_bins):
        sizes = (
            mesh.shape["cell"],
            mesh.shape["bini"],
            mesh.shape["binj"],
            contacts.shape[0],
            first_bins.shape[1],
            second_bins.shape[1],
        )
        return jax.shard_map(
            functools.partial(per_device, sizes),
            mesh=mesh,
            in_specs=placed,
            out_specs=(
                P(None, "cell"),
                P(None, ("bini", "cell", "binj")),
                P(None, ("binj", "cell", "bini")),
            ),
            check_vma=False,
        )(contacts, first_bins, second_bins)

    return whole
```

time: 629 us -> 62.8 us (0.10)
  blocking collectives: 590 us -> 0 us
  Pallas kernels: 0 us -> 56 us
  other arithmetic: 16.5 us -> 0 us
  matrix products: 14 us -> 0 us
    psum x3 -> x0, blocking collectives: 220 us -> none  [the longest x2 147 us: total_gram(): return lax.psum(gram_of(factor), ('cell', 'bini', 'binj'))]
    all_gather x4 -> x0, blocking collectives: 192 us -> none  [the longest x2 133 us: gather_second(): return lax.all_gather(factor, ('cell', 'bini'), axis=1, tiled=True)]
    unnamed x2 -> x0, blocking collectives: 178 us -> none
    pallas_call x0 -> x1, Pallas kernels: none -> 56 us  [per_device(): pl.pallas_call(functools.partial(kernel, sizes), out_shape=(jax.ShapeDtyp...]
    another operation x15 -> x0, other arithmetic: 16 us -> none  [the longest x9 8.59 us: normal_solve(): factor_low = jnp.linalg.cholesky(system)]
    dot_general x7 -> x0, matrix products: 12.8 us -> none  [the longest x1 7.09 us: one_sweep(): lax.dot_general(second_block, contacts, (((1,), (2,)), ((), ())), precisi...]
where the time goes in v1:
time: 62.8 us; the launch traced here: 62.6 us
  Pallas kernels  56 us (89%)
  local copies, waits for them, and re-layouts  5.9 us (9%)
  between operations  0.64 us (1%)
    pallas_call x1, Pallas kernels, per_device(): pl.pallas_call(functools.partial(kernel, sizes), out_shape=(jax.ShapeDtyp...  56 us
    unnamed x4, local copies, waits for them, and re-layouts  3.88 us
    pallas_call x3, local copies, waits for them, and re-layouts, per_device(): pl.pallas_call(functools.partial(kernel, sizes), out_shape=(jax.ShapeDtyp...  2.02 us

profile of v1, /device:TPU:1, one launch (start us, length us, event | category | flops | bytes accessed | tf_op | source)
XLA Modules:
  0.0 62.6 jit_solution(2930604398814230709)
XLA Ops:
  0.6 0.8 %copy.6.first_in = f32[24,12]{1,0:T(8,128)S(1)} copy(f32[24,12]{0,1:T(8,128)} %param.4) | data formatting | bytes 2304 | tf_op args[1]
  1.4 0.8 %copy.7.second_in = f32[24,12]{1,0:T(8,128)S(1)} copy(f32[24,12]{0,1:T(8,128)} %param.5) | data formatting | bytes 2304 | tf_op args[2]
  2.2 0.0 copy-start
  2.2 2.3 %copy-done = f32[16,192,384]{2,1,0:T(8,128)S(1)} copy-done((f32[16,192,384]{2,1,0:T(8,128)S(1)}, f32[16,192,384]{2,1,0:T(8,128)}, u32[]{:S(2)}) %copy-start) | copy-done | bytes 4718616
  4.5 56.0 %sweep.1 = (f32[24,16]{1,0:T(8,128)S(1)}, f32[24,12]{1,0:T(8,128)S(1)}, f32[24,12]{1,0:T(8,128)S(1)}) custom-call(f32[16,192,384]{2,1,0:T(8,128)S(1)} %copy-done, f32[24,12]{1,0:T(8,128)S(1)} %copy.6.first_in, f32[24,12]{1,0:T(8,128)S(1)} %copy.7.second_in), custom_call_target="tpu_custom_call" | custom-call | tf_op jit(solution)/shard_map/sweep/pallas_call | solution.py:484
  60.6 0.7 %copy.8 = f32[24,16]{0,1:T(8,128)} copy(f32[24,16]{1,0:T(8,128)S(1)} %get-tuple-element.3) | data formatting | bytes 3072 | tf_op jit(solution)/shard_map/sweep/pallas_call | solution.py:484
  61.2 0.7 %copy.9 = f32[24,12]{0,1:T(8,128)} copy(f32[24,12]{1,0:T(8,128)S(1)} %get-tuple-element.4) | data formatting | bytes 2304 | tf_op jit(solution)/shard_map/sweep/pallas_call | solution.py:484
  61.9 0.7 %copy.10 = f32[24,12]{0,1:T(8,128)} copy(f32[24,12]{1,0:T(8,128)S(1)} %get-tuple-element.5) | data formatting | bytes 2304 | tf_op jit(solution)/shard_map/sweep/pallas_call | solution.py:484
Async XLA Ops:
  2.2 2.3 %copy-start = (f32[16,192,384]{2,1,0:T(8,128)S(1)}, f32[16,192,384]{2,1,0:T(8,128)}, u32[]{:S(2)}) copy-start(f32[16,192,384]{2,1,0:T(8,128)} %contacts.1) | copy-start | bytes 14155780

commit v2 on v1

--- a/solution.py
+++ b/solution.py
@@ -63,9 +63,12 @@
 
 def spread(tile_at, count, width, tiles):
     lane = lanes((8, 128))
+    wholes = []
+    for v in range(count // 2):
+        wholes.extend(whole_pair(tile_at(v), SPREAD // 2))
     out = [[jnp.zeros((8, 128), jnp.float32) for _ in range(tiles)] for _ in range(G)]
     for o in range(count):
-        tile = tile_at(o)
+        tile = wholes[o]
         start = width * o
         for t in range(tiles):
             low, high = max(start, 128 * t), min(start + width, 128 * t + 128)
@@ -77,24 +80,27 @@
     return [stack([turn(out[q][t], -SPREAD * q) for q in range(G)]) for t in range(tiles)]
 
 
-def owner_tiles(tiles, count, width):
-    lane = lanes((8, 128))
-    moved = [[turn(group(tile, q), SPREAD * q) for tile in tiles] for q in range(G)]
-    out = []
-    for o in range(count):
-        start = width * o
-        packed = None
-        for q in range(G):
-            for t in range(len(tiles)):
-                low, high = max(start, 128 * t), min(start + width, 128 * t + 128)
-                if low >= high:
-                    continue
-                if packed is None:
-                    packed = moved[q][t]
-                else:
-                    packed = jnp.where(within(lane, (low + SPREAD * q) % 128, high - low), moved[q][t], packed)
-        out.append(packed)
-    return out
+def swap(tile):
+    return pltpu.roll(tile, 4, 0)
+
+
+def two(slots, v):
+    return jnp.concatenate([slots[2 * v], slots[2 * v + 1]], axis=0)
+
+
+def halve(tile, step):
+    return (tile + turn(swap(tile), step))[:4]
+
+
+def whole_pair(tile, step):
+    upper = lax.broadcasted_iota(jnp.int32, (8, 128), 0) < 4
+    swapped = swap(tile)
+    return jnp.where(upper, tile, turn(swapped, -step)), jnp.where(upper, swapped, turn(tile, -step))
+
+
+def flip(value):
+    tall = jnp.concatenate([value, jnp.zeros((128 - R, 128), jnp.float32)], axis=0)
+    return tall.T[:, :R]
 
 
 def split(value):
@@ -149,16 +155,13 @@
     contacts,
     first_in,
     second_in,
-    cell_out,
-    first_out,
-    second_out,
+    out,
     x_full,
     x_high,
     x_low,
     first_land,
     second_land,
-    first_pad,
-    second_pad,
+    pad,
     first_slots,
     second_slots,
     terms_z,
@@ -170,10 +173,10 @@
     halves_z,
     solved,
     raw_xy,
-    owned_out,
-    owned_in,
-    norms_xy,
-    norms_z,
+    parts,
+    part_in,
+    parts_xy,
+    norms,
     load_sem,
     send_sem,
     recv_sem,
@@ -185,6 +188,7 @@
     in_cz, in_cxy = c * B + b, c * A + a
     other = (1 - c, a, b)
     lane8, lane24 = lanes((8, 128)), lanes((R, 128))
+    upper8 = lax.broadcasted_iota(jnp.int32, (8, 128), 0) < 4
 
     loads = [
         pltpu.make_async_copy(second_in, second_land, load_sem.at[0]),
@@ -228,14 +232,15 @@
     lax.fori_loop(1, A, greet_cxy, 0)
     lax.fori_loop(A + 1, C * A, greet_cxy, 0)
 
-    second_pad[...] = jnp.zeros_like(second_pad)
-    first_pad[...] = jnp.zeros_like(first_pad)
+    pad[...] = jnp.zeros_like(pad)
     loads[0].wait()
-    second_pad[:, :width_second] = second_land[...]
+    pad[:width_second, :R] = second_land[...]
+    packed = pack(pad[...].T[:R], SPREAD, lax.rem(width_second * in_cxy, 128))
+    second_slots[in_cxy] = halve(packed, SPREAD // 2)
     loads[1].wait()
-    first_pad[:, :width_first] = first_land[...]
-    second_slots[in_cxy] = pack(second_pad[...], SPREAD, lax.rem(width_second * in_cxy, 128))
-    first_slots[in_cz] = pack(first_pad[...], SPREAD, lax.rem(width_first * in_cz, 128))
+    pad[:width_first, :R] = first_land[...]
+    packed = pack(pad[...].T[:R], SPREAD, lax.rem(width_first * in_cz, 128))
+    first_slots[in_cz] = halve(packed, SPREAD // 2)
 
     def send(source, target, number, device):
         pltpu.make_async_remote_copy(
@@ -273,10 +278,10 @@
     lax.fori_loop(cells // 2, cells, split_cell, 0)
 
     arrived(second_slots.at[pl.ds(0, C * A - 1)], 0)
-    second = spread(lambda o: second_slots[o], C * A, width_second, 3)
+    second = spread(lambda v: two(second_slots, v), C * A, width_second, 3)
     second_rows = split_rows(jnp.concatenate(second, axis=1))
     arrived(first_slots.at[pl.ds(0, C * B - 1)], 1)
-    first = spread(lambda o: first_slots[o], C * B, width_first, 2)
+    first = spread(lambda v: two(first_slots, v), C * B, width_first, 2)
     first_turned = [turn(group(first[0], q), 64) for q in range(G)]
     first_turned = stack(first_turned)
     last_turned = stack([turn(group(first[1], q), 64) for q in range(G)])
@@ -310,7 +315,7 @@
     summed = terms_z[0]
     for o in range(1, B):
         summed = summed + terms_z[o]
-    terms_xy[in_cxy] = jnp.where(lane8 < G * cells, summed, 0.0)
+    terms_xy[in_cxy] = halve(jnp.where(lane8 < G * cells, summed, 0.0), G * cells)
     mine = terms_xy.at[in_cxy]
     send_all(mine, mine, 4, cxy_partner, C * A)
 
@@ -328,7 +333,8 @@
         summed = terms_xy[core * A]
         for o in range(1, A):
             summed = summed + terms_xy[core * A + o]
-        block = unpack(summed, cells, cells)
+        summed = jnp.concatenate([summed, summed], axis=0)
+        block = unpack(jnp.where(upper8, summed, turn(summed, -G * cells)), cells, cells)
         block = stack([turn(group(block, q), cells * core) for q in range(G)])
         cell_total = block if cell_total is None else cell_total + block
 
@@ -336,7 +342,6 @@
     scale = jnp.sqrt(jnp.sum(unscaled * unscaled, axis=1, keepdims=True) / I + EPSILON)
     cell_factor = unscaled / scale
     own_cells = stack([turn(group(cell_factor, q), lax.rem(128 - cells * c, 128)) for q in range(G)])
-    cell_out[...] = own_cells[:, :cells]
 
     pair_sum = [jnp.zeros((R, 128), jnp.float32) for _ in range(3)]
     weights = []
@@ -360,6 +365,7 @@
     raw = gram([unscaled])
     scale_column, scale_row = diagonal_scales(raw, I)
     gram_cells = jnp.where(lane24 < R, raw / (scale_column * scale_row), 0.0)
+    out[:cells, :] = flip(own_cells)[:cells]
 
     arrived(half_in, 5)
     halves_z[b] = halves[c] + half_in[...]
@@ -394,20 +400,28 @@
         total = both if total is None else total + both
     total = total[:R] + total[R:]
 
-    tiles = owner_tiles([total[:, 128 * t : 128 * t + 128] for t in range(3)], C * A, width_second)
-    for o in range(C * A):
-        owned_out[o] = tiles[o]
-
-    def send_owned(k, carry):
-        goal = lax.rem(c + k // A, C) * A + lax.rem(a + lax.rem(k, A), A)
-        send(owned_out.at[goal], owned_in.at[k - 1], 8, cxy_partner(k))
-        return carry
-
-    lax.fori_loop(1, C * A, send_owned, 0)
-
-    raw_xy[a] = pack(gram([low, high]), R)
+    tiles = [total[:, 128 * t : 128 * t + 128] for t in range(3)]
+    middle = half_turn(tiles[1])
+    joined = half_turn(tiles[2])
+    blocks = (
+        (tiles[0], jnp.where(lane24 < 64, tiles[1], 0.0)),
+        (jnp.where(lane24 < 64, middle, joined), jnp.where(lane24 < 64, joined, 0.0)),
+    )
+    for core in range(2):
+        low, high = blocks[core]
+        parts[core, :R] = low
+        parts[core, R : R + 8] = group(high, 0) + turn(group(high, 1), 64)
+        parts[core, R + 8 :] = group(high, 2)
+    send(parts.at[1 - c], part_in, 8, other)
+
+    raw_xy[a] = pack(gram([solved[0], solved[1]]), R)
     mine = raw_xy.at[a]
     send_all(mine, mine, 9, xy_partner, A)
+    arrived(part_in, 8)
+    parts_xy[a] = parts[c] + part_in[...]
+    mine = parts_xy.at[a]
+    send_all(mine, mine, 10, xy_partner, A)
+
     arrived(raw_xy.at[pl.ds(0, A - 1)], 9)
     summed = raw_xy[0]
     for o in range(1, A):
@@ -415,48 +429,41 @@
     raw = unpack(summed, R, R)
     scale_column, scale_row = diagonal_scales(raw, J)
     gram_first = jnp.where(lane24 < R, raw / (scale_column * scale_row), 0.0)
-    system = inverse(gram_cells * gram_first)
+    system = inverse(gram_cells * gram_first) / scale_row
     start = width_first * in_cz
     at_low = lax.rem(256 - start, 128)
-    piece = stack(
-        [
-            jnp.where(
-                lane8 < 128 - start,
-                turn(group(low, q), at_low),
-                turn(group(high, q), at_low),
-            )
-            for q in range(G)
-        ]
-    )
-    first_out[...] = (piece / scale_column)[:, :width_first]
-
-    arrived(owned_in, 8)
-    summed = owned_out[in_cxy]
-    for o in range(C * A - 1):
-        summed = summed + owned_in[o]
-    second_terms = unpack(summed, SPREAD, width_second, lax.rem(width_second * in_cxy, 128))
-    unscaled = apply(system, second_terms / scale_column)
-
-    norm = jnp.sum(unscaled * unscaled, axis=1, keepdims=True)
-    norm_tile = jnp.zeros((8, 128), jnp.float32)
-    for q in range(G):
-        norm_tile = jnp.where(lane8 == q, group(norm, q), norm_tile)
-    norms_xy[in_cxy] = norm_tile
-    mine = norms_xy.at[in_cxy]
-    send_all(mine, mine, 10, cxy_partner, C * A)
-    arrived(norms_xy.at[pl.ds(0, C * A - 1)], 10)
-    summed = norms_xy[0]
-    for o in range(1, C * A):
-        summed = summed + norms_xy[o]
-    norms_z[b] = summed
-    mine = norms_z.at[b]
-    send_all(mine, mine, 11, z_partner, B)
-    arrived(norms_z.at[pl.ds(0, B - 1)], 11)
-    summed = norms_z[0]
-    for o in range(1, B):
-        summed = summed + norms_z[o]
-    norm = stack([summed[:, q : q + 1] for q in range(G)])
-    second_out[...] = (unscaled / jnp.sqrt(norm / K + EPSILON))[:, :width_second]
+    piece = [
+        jnp.where(lane8 < 128 - start, turn(group(solved[0], q), at_low), turn(group(solved[1], q), at_low))
+        for q in range(G)
+    ]
+    out[cells : cells + width_first, :] = flip(stack(piece) / scale_column)[:width_first]
+
+    arrived(parts_xy.at[pl.ds(0, A - 1)], 10)
+    summed = parts_xy[0]
+    for o in range(1, A):
+        summed = summed + parts_xy[o]
+    mixed = summed[R : R + 8]
+    low = summed[:R]
+    high = [jnp.where(lane8 < 64, mixed, 0.0), jnp.where(lane8 < 64, turn(mixed, 64), 0.0), summed[R + 8 :]]
+    low, high = apply(system, low), apply(system, stack(high))
+
+    norm = jnp.sum(low * low + high * high, axis=1, keepdims=True)
+    row24 = lax.broadcasted_iota(jnp.int32, (R, 128), 0)
+    norms[in_cz] = jnp.sum(jnp.where(lane24 == row24, norm, 0.0), axis=0, keepdims=True)
+    mine = norms.at[in_cz]
+    send_all(mine, mine, 11, cz_partner, C * B)
+    start = width_second * a
+    at_low = lax.rem(256 - start, 128)
+    piece = [
+        jnp.where(lane8 < 128 - start, turn(group(low, q), at_low), turn(group(high, q), at_low))
+        for q in range(G)
+    ]
+    piece = flip(stack(piece))[:width_second]
+    arrived(norms.at[pl.ds(0, C * B - 1)], 11)
+    norm = norms[0]
+    for o in range(1, C * B):
+        norm = norm + norms[o]
+    out[cells + 16 : cells + 16 + width_second, :] = piece / jnp.sqrt(norm / K + EPSILON)[:, :R]
 
     left(second_slots.at[pl.ds(0, C * A - 1)], 0)
     left(first_slots.at[pl.ds(0, C * B - 1)], 1)
@@ -466,10 +473,21 @@
     left(half_in, 5)
     left(halves_z.at[pl.ds(0, B - 1)], 6)
     left(solved.at[0], 7)
-    left(owned_in, 8)
+    left(part_in, 8)
     left(raw_xy.at[pl.ds(0, A - 1)], 9)
-    left(norms_xy.at[pl.ds(0, C * A - 1)], 10)
-    left(norms_z.at[pl.ds(0, B - 1)], 11)
+    left(parts_xy.at[pl.ds(0, A - 1)], 10)
+    left(norms.at[pl.ds(0, C * B - 1)], 11)
+
+
+def share(counts, out, cells, first, second, sem):
+    copies = [
+        pltpu.make_async_copy(out.at[pl.ds(16 * n, counts[n])], target, sem.at[n])
+        for n, target in enumerate((cells, first, second))
+    ]
+    for copy in copies:
+        copy.start()
+    for copy in copies:
+        copy.wait()
 
 
 def per_device(sizes, contacts, first_bins, second_bins):
@@ -480,49 +498,55 @@
     def tiles(*lead):
         return pltpu.VMEM(lead + (8, 128), f32)
 
-    return tuple(
+    first_bins, second_bins = first_bins.T, second_bins.T
+    out = (
         pl.pallas_call(
             functools.partial(kernel, sizes),
-            out_shape=(
-                jax.ShapeDtypeStruct((R, cells), f32),
-                jax.ShapeDtypeStruct(first_bins.shape, f32),
-                jax.ShapeDtypeStruct(second_bins.shape, f32),
-            ),
+            out_shape=jax.ShapeDtypeStruct((cells + 32, R), f32),
             in_specs=[pl.BlockSpec(memory_space=pl.ANY)] * 3,
-            out_specs=[pl.BlockSpec(memory_space=pltpu.VMEM)] * 3,
+            out_specs=pl.BlockSpec(memory_space=pltpu.VMEM),
             scratch_shapes=[
                 pltpu.VMEM((cells, rows, columns), f32),
                 pltpu.VMEM((cells * rows, columns), jnp.bfloat16),
                 pltpu.VMEM((cells * rows, columns), jnp.bfloat16),
                 pltpu.VMEM(first_bins.shape, f32),
                 pltpu.VMEM(second_bins.shape, f32),
-                pltpu.VMEM((R, 128), f32),
-                pltpu.VMEM((R, 128), f32),
-                tiles(C * B),
-                tiles(C * A),
+                pltpu.VMEM((128, 128), f32),
+                pltpu.VMEM((C * B, 4, 128), f32),
+                pltpu.VMEM((C * A, 4, 128), f32),
                 tiles(B),
                 tiles(A),
-                tiles(C * A),
+                pltpu.VMEM((C * A, 4, 128), f32),
                 pltpu.VMEM((cells // 2, R, 2 * rows), f32),
                 pltpu.VMEM((2, R, 128), f32),
                 pltpu.VMEM((R, 128), f32),
                 pltpu.VMEM((B, R, 128), f32),
                 pltpu.VMEM((2, R, 128), f32),
                 tiles(A),
-                tiles(C * A),
-                tiles(C * A - 1),
-                tiles(C * A),
-                tiles(B),
+                pltpu.VMEM((2, R + 16, 128), f32),
+                pltpu.VMEM((R + 16, 128), f32),
+                pltpu.VMEM((A, R + 16, 128), f32),
+                pltpu.VMEM((C * B, 1, 128), f32),
                 pltpu.SemaphoreType.DMA((2 + cells,)),
                 pltpu.SemaphoreType.DMA((12,)),
                 pltpu.SemaphoreType.DMA((12,)),
             ],
             compiler_params=pltpu.CompilerParams(
-                collective_id=0, has_side_effects=True, vmem_limit_bytes=40 * 1024 * 1024
+                collective_id=0, has_side_effects=True, vmem_limit_bytes=60 * 1024 * 1024
             ),
             name="sweep",
         )(contacts, first_bins, second_bins)
     )
+    counts = (cells, first_bins.shape[0], second_bins.shape[0])
+    shares = pl.pallas_call(
+        functools.partial(share, counts),
+        out_shape=tuple(jax.ShapeDtypeStruct((n, R), f32) for n in counts),
+        in_specs=[pl.BlockSpec(memory_space=pl.ANY)],
+        out_specs=[pl.BlockSpec(memory_space=pl.ANY)] * 3,
+        scratch_shapes=[pltpu.SemaphoreType.DMA((3,))],
+        name="share",
+    )(out)
+    return tuple(piece.T for piece in shares)
 
 
 def solution(mesh):

time: 62.8 us -> 52 us (0.83)
  local copies, waits for them, and re-layouts: 5.9 us -> 0 us
  Pallas kernels: 56 us -> 51.3 us
    pallas_call x1 -> x2, Pallas kernels: 56 us -> 51.3 us  [the longest x1 49.5 us: per_device(): pl.pallas_call(functools.partial(kernel, sizes), out_shape=jax.ShapeDtype...]
    unnamed x4 -> x0, local copies, waits for them, and re-layouts: 3.88 us -> none
    pallas_call x3 -> x0, local copies, waits for them, and re-layouts: 2.02 us -> none  [per_device(): pl.pallas_call(functools.partial(kernel, sizes), out_shape=(jax.ShapeDtyp...]
where the time goes in v2:
time: 52 us; the launch traced here: 51.9 us
  Pallas kernels  51.3 us (99%)
  between operations  0.64 us (1%)
    pallas_call x1, Pallas kernels, per_device(): pl.pallas_call(functools.partial(kernel, sizes), out_shape=jax.ShapeDtype...  49.5 us
    pallas_call x1, Pallas kernels, per_device(): pl.pallas_call(functools.partial(share, counts), out_shape=tuple((jax.Sha...  1.75 us

profile of v2, /device:TPU:1, one launch (start us, length us, event | category | flops | bytes accessed | tf_op | source)
XLA Modules:
  0.0 51.9 jit_solution(10783514244009822006)
XLA Ops:
  0.6 49.5 %sweep.1.out = f32[48,24]{1,0:T(8,128)} custom-call(f32[16,192,384]{2,1,0:T(8,128)} %contacts.1, f32[12,24]{1,0:T(8,128)} %bitcast.5, f32[12,24]{1,0:T(8,128)} %bitcast.6), custom_call_target="tpu_custom_call" | custom-call | tf_op jit(solution)/shard_map/sweep/pallas_call | solution.py:503
  50.2 1.8 %share.1 = (f32[16,24]{1,0:T(8,128)}, f32[12,24]{1,0:T(8,128)}, f32[12,24]{1,0:T(8,128)}) custom-call(f32[48,24]{1,0:T(8,128)} %sweep.1.out), custom_call_target="tpu_custom_call" | custom-call | tf_op jit(solution)/shard_map/share/pallas_call | solution.py:541

commit v3 on v2

--- a/solution.py
+++ b/solution.py
@@ -134,10 +134,15 @@
     return a
 
 
-def apply(matrix, value):
+def widen(matrix, wide):
+    for s in range(R):
+        wide[s] = jnp.broadcast_to(matrix[:, s : s + 1], (R, 128))
+
+
+def apply(wide, value):
     total = None
     for s in range(R):
-        term = matrix[:, s : s + 1] * value[s : s + 1, :]
+        term = wide[s] * value[s : s + 1, :]
         total = term if total is None else total + term
     return total
 
@@ -157,8 +162,8 @@
     second_in,
     out,
     x_full,
-    x_high,
-    x_low,
+    x_parts,
+    x_turned,
     first_land,
     second_land,
     pad,
@@ -177,12 +182,13 @@
     part_in,
     parts_xy,
     norms,
+    wide_system,
     load_sem,
     send_sem,
     recv_sem,
 ):
     C, A, B, I, J, K = sizes
-    cells, rows = x_full.shape[0], x_full.shape[1]
+    cells, rows, columns = x_full.shape
     width_first, width_second = rows // (C * B), x_full.shape[2] // (C * A)
     c, a, b = lax.axis_index("cell"), lax.axis_index("bini"), lax.axis_index("binj")
     in_cz, in_cxy = c * B + b, c * A + a
@@ -190,6 +196,43 @@
     lane8, lane24 = lanes((8, 128)), lanes((R, 128))
     upper8 = lax.broadcasted_iota(jnp.int32, (8, 128), 0) < 4
 
+    barrier = pltpu.get_barrier_semaphore()
+
+    def signal(device):
+        pl.semaphore_signal(barrier, inc=1, device_id=device, device_id_type=MESH)
+
+    def flipped(m, size):
+        first = size // 2 if size == B else size // 2 + size // 8
+        m = m + first
+        return jnp.where(m >= size, m - size + 1, m)
+
+    def z_partner(m):
+        return (c, a, b ^ flipped(m, B))
+
+    def xy_partner(m):
+        return (c, a ^ flipped(m, A), b)
+
+    def across(device):
+        return (1 - c, device[1], device[2])
+
+    def over(count, partner, both, action):
+        def one(m, carry):
+            device = partner(m)
+            action(device)
+            if both:
+                action(across(device))
+            return carry
+
+        lax.fori_loop(0, count - 1, one, 0)
+        if both:
+            action(other)
+
+    z_partners, cz_partners = (B, z_partner, False), (B, z_partner, True)
+    xy_partners, cxy_partners = (A, xy_partner, False), (A, xy_partner, True)
+    over(*cxy_partners, signal)
+    over(B, z_partner, False, signal)
+    over(B, lambda m: across(z_partner(m)), False, signal)
+
     loads = [
         pltpu.make_async_copy(second_in, second_land, load_sem.at[0]),
         pltpu.make_async_copy(first_in, first_land, load_sem.at[1]),
@@ -202,35 +245,6 @@
 
     for i in range(cells):
         load_cell(i).start()
-
-    barrier = pltpu.get_barrier_semaphore()
-
-    def signal(device):
-        pl.semaphore_signal(barrier, inc=1, device_id=device, device_id_type=MESH)
-
-    def z_partner(k):
-        return (c, a, lax.rem(b + k, B))
-
-    def xy_partner(k):
-        return (c, lax.rem(a + k, A), b)
-
-    def cz_partner(k):
-        return (lax.rem(c + k // B, C), a, lax.rem(b + lax.rem(k, B), B))
-
-    def cxy_partner(k):
-        return (lax.rem(c + k // A, C), lax.rem(a + lax.rem(k, A), A), b)
-
-    def greet_cz(k, carry):
-        signal(cz_partner(k))
-        return carry
-
-    def greet_cxy(k, carry):
-        signal(cxy_partner(k))
-        return carry
-
-    lax.fori_loop(1, C * B, greet_cz, 0)
-    lax.fori_loop(1, A, greet_cxy, 0)
-    lax.fori_loop(A + 1, C * A, greet_cxy, 0)
 
     pad[...] = jnp.zeros_like(pad)
     loads[0].wait()
@@ -247,12 +261,8 @@
             source, target, send_sem.at[number], recv_sem.at[number], device_id=device, device_id_type=MESH
         ).start()
 
-    def send_all(source, target, number, partner, count):
-        def one(k, carry):
-            send(source, target, number, partner(k))
-            return carry
-
-        lax.fori_loop(1, count, one, 0)
+    def send_all(source, target, number, partners):
+        over(*partners, lambda device: send(source, target, number, device))
 
     def arrived(like, number):
         pltpu.make_async_copy(like, like, recv_sem.at[number]).wait()
@@ -260,26 +270,27 @@
     def left(like, number):
         pltpu.make_async_copy(like, like, send_sem.at[number]).wait()
 
-    def split_cell(i, carry):
-        load_cell(i).wait()
-        high, low = split(x_full[i])
-        at = pl.ds(pl.multiple_of(i * rows, rows), rows)
-        x_high[at, :] = high
-        x_low[at, :] = low
+    def split_pair(p, carry):
+        load_cell(2 * p).wait()
+        load_cell(2 * p + 1).wait()
+        pair = x_full[pl.ds(2 * p, 2)].reshape(2 * rows, columns)
+        at = pl.ds(pl.multiple_of(2 * rows * p, 2 * rows), 2 * rows)
+        x_parts[at, :columns], x_parts[at, columns:] = split(pair)
+        x_turned[:columns, at], x_turned[columns:, at] = split(pair.T)
         return carry
 
-    lax.fori_loop(0, cells // 2, split_cell, 0)
     pl.semaphore_wait(barrier, C * B - 1 + C * (A - 1))
 
     mine = second_slots.at[in_cxy]
-    send_all(mine, mine, 0, cxy_partner, C * A)
+    send_all(mine, mine, 0, cxy_partners)
     mine = first_slots.at[in_cz]
-    send_all(mine, mine, 1, cz_partner, C * B)
-    lax.fori_loop(cells // 2, cells, split_cell, 0)
+    send_all(mine, mine, 1, cz_partners)
+    lax.fori_loop(0, cells // 2, split_pair, 0)
 
     arrived(second_slots.at[pl.ds(0, C * A - 1)], 0)
     second = spread(lambda v: two(second_slots, v), C * A, width_second, 3)
     second_rows = split_rows(jnp.concatenate(second, axis=1))
+    second_rows = jnp.concatenate([second_rows, second_rows], axis=1)
     arrived(first_slots.at[pl.ds(0, C * B - 1)], 1)
     first = spread(lambda v: two(first_slots, v), C * B, width_first, 2)
     first_turned = [turn(group(first[0], q), 64) for q in range(G)]
@@ -293,10 +304,11 @@
 
     cell_terms = jnp.zeros((R, 128), jnp.float32)
     for p in range(cells // 2):
-        at = pl.ds(2 * rows * p, 2 * rows)
-        big = lax.dot_general(second_rows, x_high[at, :], NT, preferred_element_type=jnp.float32)
-        small = lax.dot_general(second_rows, x_low[at, :], NT, preferred_element_type=jnp.float32)
-        both = (small[:R] + small[R:]) + big[R:] + big[:R]
+        if p % 2 == 0:
+            at = pl.ds(2 * rows * p, 4 * rows)
+            wide = jnp.dot(second_rows, x_turned[:, at], preferred_element_type=jnp.float32)
+            wide = wide[:R] + wide[R:]
+        both = wide[:, 2 * rows * (p % 2) : 2 * rows * (p % 2 + 1)]
         products[p] = both
         terms = [both[:, 128 * t : 128 * t + 128] * first_pair[t] for t in range(3)]
         even = jnp.sum(terms[0] + jnp.where(lane24 < 64, terms[1], 0.0), axis=1, keepdims=True)
@@ -306,10 +318,10 @@
 
     terms_z[b] = pack(cell_terms, cells) + turn(pack(gram(second), R), 56)
     mine = terms_z.at[b]
-    send_all(mine, mine, 2, z_partner, B)
+    send_all(mine, mine, 2, z_partners)
     grams_xy[a] = pack(gram(first), R)
     mine = grams_xy.at[a]
-    send_all(mine, mine, 3, xy_partner, A)
+    send_all(mine, mine, 3, xy_partners)
 
     arrived(terms_z.at[pl.ds(0, B - 1)], 2)
     summed = terms_z[0]
@@ -317,7 +329,7 @@
         summed = summed + terms_z[o]
     terms_xy[in_cxy] = halve(jnp.where(lane8 < G * cells, summed, 0.0), G * cells)
     mine = terms_xy.at[in_cxy]
-    send_all(mine, mine, 4, cxy_partner, C * A)
+    send_all(mine, mine, 4, cxy_partners)
 
     gram_second = unpack(turn(summed, -56), R, R)
     arrived(grams_xy.at[pl.ds(0, A - 1)], 3)
@@ -325,7 +337,7 @@
     for o in range(1, A):
         summed = summed + grams_xy[o]
     gram_first = unpack(summed, R, R)
-    system = inverse(gram_first * gram_second)
+    widen(inverse(gram_first * gram_second), wide_system)
 
     arrived(terms_xy.at[pl.ds(0, C * A - 1)], 4)
     cell_total = None
@@ -338,7 +350,7 @@
         block = stack([turn(group(block, q), cells * core) for q in range(G)])
         cell_total = block if cell_total is None else cell_total + block
 
-    unscaled = apply(system, cell_total)
+    unscaled = apply(wide_system, cell_total)
     scale = jnp.sqrt(jnp.sum(unscaled * unscaled, axis=1, keepdims=True) / I + EPSILON)
     cell_factor = unscaled / scale
     own_cells = stack([turn(group(cell_factor, q), lax.rem(128 - cells * c, 128)) for q in range(G)])
@@ -362,21 +374,20 @@
     halves[1] = jnp.where(lane24 < 64, pair_sum[1] + turned[1], 0.0)
     send(halves.at[1 - c], half_in, 5, other)
 
+    arrived(half_in, 5)
+    halves_z[b] = halves[c] + half_in[...]
+    mine = halves_z.at[b]
+    send_all(mine, mine, 6, z_partners)
     raw = gram([unscaled])
     scale_column, scale_row = diagonal_scales(raw, I)
     gram_cells = jnp.where(lane24 < R, raw / (scale_column * scale_row), 0.0)
     out[:cells, :] = flip(own_cells)[:cells]
-
-    arrived(half_in, 5)
-    halves_z[b] = halves[c] + half_in[...]
-    mine = halves_z.at[b]
-    send_all(mine, mine, 6, z_partner, B)
-    system = inverse(gram_cells * gram_second)
+    widen(inverse(gram_cells * gram_second), wide_system)
     arrived(halves_z.at[pl.ds(0, B - 1)], 6)
     summed = halves_z[0]
     for o in range(1, B):
         summed = summed + halves_z[o]
-    solved[c] = apply(system, summed)
+    solved[c] = apply(wide_system, summed)
     mine = solved.at[c]
     send(mine, mine, 7, other)
     arrived(solved.at[0], 7)
@@ -389,15 +400,13 @@
         jnp.where(lane24 < 64, low_turned, high_turned),
     ]
     total = None
-    for p in range(cells // 2):
-        at = pl.ds(2 * rows * p, 2 * rows)
+    for p in range(0, cells // 2, 2):
         left_rows = split_rows(
-            jnp.concatenate([solved_pair[t] * weights[p][t] for t in range(3)], axis=1)
+            jnp.concatenate([solved_pair[t] * weights[p + h][t] for h in range(2) for t in range(3)], axis=1)
         )
-        big = jnp.dot(left_rows, x_high[at, :], preferred_element_type=jnp.float32)
-        small = jnp.dot(left_rows, x_low[at, :], preferred_element_type=jnp.float32)
-        both = big + small
+        both = jnp.dot(left_rows, x_parts[pl.ds(2 * rows * p, 4 * rows), :], preferred_element_type=jnp.float32)
         total = both if total is None else total + both
+    total = total[:, :columns] + total[:, columns:]
     total = total[:R] + total[R:]
 
     tiles = [total[:, 128 * t : 128 * t + 128] for t in range(3)]
@@ -416,11 +425,11 @@
 
     raw_xy[a] = pack(gram([solved[0], solved[1]]), R)
     mine = raw_xy.at[a]
-    send_all(mine, mine, 9, xy_partner, A)
+    send_all(mine, mine, 9, xy_partners)
     arrived(part_in, 8)
     parts_xy[a] = parts[c] + part_in[...]
     mine = parts_xy.at[a]
-    send_all(mine, mine, 10, xy_partner, A)
+    send_all(mine, mine, 10, xy_partners)
 
     arrived(raw_xy.at[pl.ds(0, A - 1)], 9)
     summed = raw_xy[0]
@@ -429,7 +438,7 @@
     raw = unpack(summed, R, R)
     scale_column, scale_row = diagonal_scales(raw, J)
     gram_first = jnp.where(lane24 < R, raw / (scale_column * scale_row), 0.0)
-    system = inverse(gram_cells * gram_first) / scale_row
+    widen(inverse(gram_cells * gram_first) / scale_row, wide_system)
     start = width_first * in_cz
     at_low = lax.rem(256 - start, 128)
     piece = [
@@ -445,13 +454,13 @@
     mixed = summed[R : R + 8]
     low = summed[:R]
     high = [jnp.where(lane8 < 64, mixed, 0.0), jnp.where(lane8 < 64, turn(mixed, 64), 0.0), summed[R + 8 :]]
-    low, high = apply(system, low), apply(system, stack(high))
+    low, high = apply(wide_system, low), apply(wide_system, stack(high))
 
     norm = jnp.sum(low * low + high * high, axis=1, keepdims=True)
     row24 = lax.broadcasted_iota(jnp.int32, (R, 128), 0)
     norms[in_cz] = jnp.sum(jnp.where(lane24 == row24, norm, 0.0), axis=0, keepdims=True)
     mine = norms.at[in_cz]
-    send_all(mine, mine, 11, cz_partner, C * B)
+    send_all(mine, mine, 11, cz_partners)
     start = width_second * a
     at_low = lax.rem(256 - start, 128)
     piece = [
@@ -507,8 +516,8 @@
             out_specs=pl.BlockSpec(memory_space=pltpu.VMEM),
             scratch_shapes=[
                 pltpu.VMEM((cells, rows, columns), f32),
-                pltpu.VMEM((cells * rows, columns), jnp.bfloat16),
-                pltpu.VMEM((cells * rows, columns), jnp.bfloat16),
+                pltpu.VMEM((cells * rows, 2 * columns), jnp.bfloat16),
+                pltpu.VMEM((2 * columns, cells * rows), jnp.bfloat16),
                 pltpu.VMEM(first_bins.shape, f32),
                 pltpu.VMEM(second_bins.shape, f32),
                 pltpu.VMEM((128, 128), f32),
@@ -527,6 +536,7 @@
                 pltpu.VMEM((R + 16, 128), f32),
                 pltpu.VMEM((A, R + 16, 128), f32),
                 pltpu.VMEM((C * B, 1, 128), f32),
+                pltpu.VMEM((R, R, 128), f32),
                 pltpu.SemaphoreType.DMA((2 + cells,)),
                 pltpu.SemaphoreType.DMA((12,)),
                 pltpu.SemaphoreType.DMA((12,)),

time: 52 us -> 50.3 us (0.967)
  Pallas kernels: 51.3 us -> 49.5 us
    pallas_call x1, Pallas kernels: 49.5 us -> 47.8 us  [per_device(): pl.pallas_call(functools.partial(kernel, sizes), out_shape=jax.ShapeDtype...]
where the time goes in v3:
time: 50.3 us; the launch traced here: 50.2 us
  Pallas kernels  49.5 us (98%)
  between operations  0.64 us (1%)
    pallas_call x1, Pallas kernels, per_device(): pl.pallas_call(functools.partial(kernel, sizes), out_shape=jax.ShapeDtype...  47.8 us
    pallas_call x1, Pallas kernels, per_device(): pl.pallas_call(functools.partial(share, counts), out_shape=tuple((jax.Sha...  1.75 us

profile of v3, /device:TPU:1, one launch (start us, length us, event | category | flops | bytes accessed | tf_op | source)
XLA Modules:
  0.0 50.2 jit_solution(15943681565669894731)
XLA Ops:
  0.6 47.8 %sweep.1.out = f32[48,24]{1,0:T(8,128)} custom-call(f32[16,192,384]{2,1,0:T(8,128)} %contacts.1, f32[12,24]{1,0:T(8,128)} %bitcast.5, f32[12,24]{1,0:T(8,128)} %bitcast.6), custom_call_target="tpu_custom_call" | custom-call | tf_op jit(solution)/shard_map/sweep/pallas_call | solution.py:512
  48.4 1.8 %share.1 = (f32[16,24]{1,0:T(8,128)}, f32[12,24]{1,0:T(8,128)}, f32[12,24]{1,0:T(8,128)}) custom-call(f32[48,24]{1,0:T(8,128)} %sweep.1.out), custom_call_target="tpu_custom_call" | custom-call | tf_op jit(solution)/shard_map/share/pallas_call | solution.py:551

commit v4 on v3

--- a/solution.py
+++ b/solution.py
@@ -178,6 +178,7 @@
     halves_z,
     solved,
     raw_xy,
+    left_rows,
     parts,
     part_in,
     parts_xy,
@@ -229,9 +230,9 @@
 
     z_partners, cz_partners = (B, z_partner, False), (B, z_partner, True)
     xy_partners, cxy_partners = (A, xy_partner, False), (A, xy_partner, True)
-    over(*cxy_partners, signal)
-    over(B, z_partner, False, signal)
-    over(B, lambda m: across(z_partner(m)), False, signal)
+    over(*cz_partners, signal)
+    over(A, xy_partner, False, signal)
+    over(A, lambda m: across(xy_partner(m)), False, signal)
 
     loads = [
         pltpu.make_async_copy(second_in, second_land, load_sem.at[0]),
@@ -275,7 +276,11 @@
         load_cell(2 * p + 1).wait()
         pair = x_full[pl.ds(2 * p, 2)].reshape(2 * rows, columns)
         at = pl.ds(pl.multiple_of(2 * rows * p, 2 * rows), 2 * rows)
-        x_parts[at, :columns], x_parts[at, columns:] = split(pair)
+        high = pair.astype(jnp.bfloat16).astype(jnp.float32)
+        low = pair - high
+        half = columns // 2
+        x_parts[at, :columns] = jnp.concatenate([high[:, :half], low[:, :half]], axis=1).astype(jnp.bfloat16)
+        x_parts[at, columns:] = jnp.concatenate([high[:, half:], low[:, half:]], axis=1).astype(jnp.bfloat16)
         x_turned[:columns, at], x_turned[columns:, at] = split(pair.T)
         return carry
 
@@ -392,6 +397,7 @@
     send(mine, mine, 7, other)
     arrived(solved.at[0], 7)
     low, high = solved[0], solved[1]
+    raw_xy[a] = pack(gram([low, high]), R)
 
     low_turned, high_turned = half_turn(low), half_turn(high)
     solved_pair = [
@@ -399,35 +405,32 @@
         jnp.where(lane24 < 64, high, low_turned),
         jnp.where(lane24 < 64, low_turned, high_turned),
     ]
-    total = None
     for p in range(0, cells // 2, 2):
-        left_rows = split_rows(
+        left_rows[:, 2 * rows * p : 2 * rows * (p + 2)] = split_rows(
             jnp.concatenate([solved_pair[t] * weights[p + h][t] for h in range(2) for t in range(3)], axis=1)
         )
-        both = jnp.dot(left_rows, x_parts[pl.ds(2 * rows * p, 4 * rows), :], preferred_element_type=jnp.float32)
-        total = both if total is None else total + both
-    total = total[:, :columns] + total[:, columns:]
-    total = total[:R] + total[R:]
-
-    tiles = [total[:, 128 * t : 128 * t + 128] for t in range(3)]
-    middle = half_turn(tiles[1])
-    joined = half_turn(tiles[2])
-    blocks = (
-        (tiles[0], jnp.where(lane24 < 64, tiles[1], 0.0)),
-        (jnp.where(lane24 < 64, middle, joined), jnp.where(lane24 < 64, joined, 0.0)),
-    )
-    for core in range(2):
-        low, high = blocks[core]
-        parts[core, :R] = low
-        parts[core, R : R + 8] = group(high, 0) + turn(group(high, 1), 64)
-        parts[core, R + 8 :] = group(high, 2)
-    send(parts.at[1 - c], part_in, 8, other)
-
-    raw_xy[a] = pack(gram([solved[0], solved[1]]), R)
+
+    def second_pass(core):
+        at = pl.ds(pl.multiple_of(columns * core, columns), columns)
+        total = None
+        for p in range(0, cells // 2, 2):
+            here = pl.ds(2 * rows * p, 4 * rows)
+            both = jnp.dot(left_rows[:, here], x_parts[here, at], preferred_element_type=jnp.float32)
+            total = both if total is None else total + both
+        total = total[:R] + total[R:]
+        first, middle, last = [total[:, 128 * t : 128 * t + 128] for t in range(3)]
+        middle, last = half_turn(middle), half_turn(last)
+        low = first + jnp.where(lane24 < 64, middle, last)
+        high = jnp.where(lane24 < 64, total[:, 128:256] + last, 0.0)
+        return jnp.concatenate([low, group(high, 0) + turn(group(high, 1), 64), group(high, 2)], axis=0)
+
+    parts[...] = second_pass(1 - c)
+    send(parts, part_in, 8, other)
     mine = raw_xy.at[a]
     send_all(mine, mine, 9, xy_partners)
+    own_part = second_pass(c)
     arrived(part_in, 8)
-    parts_xy[a] = parts[c] + part_in[...]
+    parts_xy[a] = own_part + part_in[...]
     mine = parts_xy.at[a]
     send_all(mine, mine, 10, xy_partners)
 
@@ -532,7 +535,8 @@
                 pltpu.VMEM((B, R, 128), f32),
                 pltpu.VMEM((2, R, 128), f32),
                 tiles(A),
-                pltpu.VMEM((2, R + 16, 128), f32),
+                pltpu.VMEM((2 * R, cells * rows), jnp.bfloat16),
+                pltpu.VMEM((R + 16, 128), f32),
                 pltpu.VMEM((R + 16, 128), f32),
                 pltpu.VMEM((A, R + 16, 128), f32),
                 pltpu.VMEM((C * B, 1, 128), f32),

time: 50.3 us -> 49.7 us (0.988)
  Pallas kernels: 49.5 us -> 48.9 us
    pallas_call x1, Pallas kernels: 47.8 us -> 47.2 us  [per_device(): pl.pallas_call(functools.partial(kernel, sizes), out_shape=jax.ShapeDtype...]
where the time goes in v4:
time: 49.7 us; the launch traced here: 49.6 us
  Pallas kernels  48.9 us (98%)
  between operations  0.64 us (1%)
    pallas_call x1, Pallas kernels, per_device(): pl.pallas_call(functools.partial(kernel, sizes), out_shape=jax.ShapeDtype...  47.2 us
    pallas_call x1, Pallas kernels, per_device(): pl.pallas_call(functools.partial(share, counts), out_shape=tuple((jax.Sha...  1.75 us

profile of v4, /device:TPU:1, one launch (start us, length us, event | category | flops | bytes accessed | tf_op | source)
XLA Modules:
  0.0 49.6 jit_solution(10981383149005867053)
XLA Ops:
  0.6 47.2 %sweep.1.out = f32[48,24]{1,0:T(8,128)} custom-call(f32[16,192,384]{2,1,0:T(8,128)} %contacts.1, f32[12,24]{1,0:T(8,128)} %bitcast.5, f32[12,24]{1,0:T(8,128)} %bitcast.6), custom_call_target="tpu_custom_call" | custom-call | tf_op jit(solution)/shard_map/sweep/pallas_call | solution.py:515
  47.8 1.8 %share.1 = (f32[16,24]{1,0:T(8,128)}, f32[12,24]{1,0:T(8,128)}, f32[12,24]{1,0:T(8,128)}) custom-call(f32[48,24]{1,0:T(8,128)} %sweep.1.out), custom_call_target="tpu_custom_call" | custom-call | tf_op jit(solution)/shard_map/share/pallas_call | solution.py:555

commit v5 on v4

--- a/solution.py
+++ b/solution.py
@@ -555,7 +555,7 @@
     shares = pl.pallas_call(
         functools.partial(share, counts),
         out_shape=tuple(jax.ShapeDtypeStruct((n, R), f32) for n in counts),
-        in_specs=[pl.BlockSpec(memory_space=pl.ANY)],
+        in_specs=[pl.BlockSpec(memory_space=pltpu.VMEM)],
         out_specs=[pl.BlockSpec(memory_space=pl.ANY)] * 3,
         scratch_shapes=[pltpu.SemaphoreType.DMA((3,))],
         name="share",

time: 49.7 us -> 49.3 us (level)
  no operation moved by 1% of the time
where the time goes in v5:
time: 49.3 us; the launch traced here: 49.2 us
  Pallas kernels  48.5 us (98%)
  between operations  0.64 us (1%)
    pallas_call x1, Pallas kernels, per_device(): pl.pallas_call(functools.partial(kernel, sizes), out_shape=jax.ShapeDtype...  47.2 us
    pallas_call x1, Pallas kernels, per_device(): pl.pallas_call(functools.partial(share, counts), out_shape=tuple((jax.Sha...  1.36 us

profile of v5, /device:TPU:1, one launch (start us, length us, event | category | flops | bytes accessed | tf_op | source)
XLA Modules:
  0.0 49.2 jit_solution(1711417653763881325)
XLA Ops:
  0.6 47.2 %sweep.1.out = f32[48,24]{1,0:T(8,128)} custom-call(f32[16,192,384]{2,1,0:T(8,128)} %contacts.1, f32[12,24]{1,0:T(8,128)} %bitcast.5, f32[12,24]{1,0:T(8,128)} %bitcast.6), custom_call_target="tpu_custom_call" | custom-call | tf_op jit(solution)/shard_map/sweep/pallas_call | solution.py:515
  47.8 1.4 %share.1 = (f32[16,24]{1,0:T(8,128)}, f32[12,24]{1,0:T(8,128)}, f32[12,24]{1,0:T(8,128)}) custom-call(f32[48,24]{1,0:T(8,128)} %sweep.1.out), custom_call_target="tpu_custom_call" | custom-call | tf_op jit(solution)/shard_map/share/pallas_call | solution.py:555

commit v6 on v5

--- a/solution.py
+++ b/solution.py
@@ -356,9 +356,7 @@
         cell_total = block if cell_total is None else cell_total + block
 
     unscaled = apply(wide_system, cell_total)
-    scale = jnp.sqrt(jnp.sum(unscaled * unscaled, axis=1, keepdims=True) / I + EPSILON)
-    cell_factor = unscaled / scale
-    own_cells = stack([turn(group(cell_factor, q), lax.rem(128 - cells * c, 128)) for q in range(G)])
+    own_cells = stack([turn(group(unscaled, q), lax.rem(128 - cells * c, 128)) for q in range(G)])
 
     pair_sum = [jnp.zeros((R, 128), jnp.float32) for _ in range(3)]
     weights = []
@@ -386,8 +384,9 @@
     raw = gram([unscaled])
     scale_column, scale_row = diagonal_scales(raw, I)
     gram_cells = jnp.where(lane24 < R, raw / (scale_column * scale_row), 0.0)
-    out[:cells, :] = flip(own_cells)[:cells]
-    widen(inverse(gram_cells * gram_second), wide_system)
+    out[:cells, :] = flip(own_cells / scale_column)[:cells]
+    cell_scales = scale_row
+    widen(inverse(gram_cells * gram_second) / cell_scales, wide_system)
     arrived(halves_z.at[pl.ds(0, B - 1)], 6)
     summed = halves_z[0]
     for o in range(1, B):
@@ -441,7 +440,7 @@
     raw = unpack(summed, R, R)
     scale_column, scale_row = diagonal_scales(raw, J)
     gram_first = jnp.where(lane24 < R, raw / (scale_column * scale_row), 0.0)
-    widen(inverse(gram_cells * gram_first) / scale_row, wide_system)
+    widen(inverse(gram_cells * gram_first) / scale_row / cell_scales, wide_system)
     start = width_first * in_cz
     at_low = lax.rem(256 - start, 128)
     piece = [
@@ -471,12 +470,6 @@
         for q in range(G)
     ]
     piece = flip(stack(piece))[:width_second]
-    arrived(norms.at[pl.ds(0, C * B - 1)], 11)
-    norm = norms[0]
-    for o in range(1, C * B):
-        norm = norm + norms[o]
-    out[cells + 16 : cells + 16 + width_second, :] = piece / jnp.sqrt(norm / K + EPSILON)[:, :R]
-
     left(second_slots.at[pl.ds(0, C * A - 1)], 0)
     left(first_slots.at[pl.ds(0, C * B - 1)], 1)
     left(terms_z.at[pl.ds(0, B - 1)], 2)
@@ -488,6 +481,11 @@
     left(part_in, 8)
     left(raw_xy.at[pl.ds(0, A - 1)], 9)
     left(parts_xy.at[pl.ds(0, A - 1)], 10)
+    arrived(norms.at[pl.ds(0, C * B - 1)], 11)
+    norm = norms[0]
+    for o in range(1, C * B):
+        norm = norm + norms[o]
+    out[cells + 16 : cells + 16 + width_second, :] = piece / jnp.sqrt(norm / K + EPSILON)[:, :R]
     left(norms.at[pl.ds(0, C * B - 1)], 11)
 
 

time: 49.3 us -> 49.2 us (level)
  no operation moved by 1% of the time
where the time goes in v6:
time: 49.2 us; the launch traced here: 49.1 us
  Pallas kernels  48.4 us (98%)
  between operations  0.64 us (1%)
    pallas_call x1, Pallas kernels, per_device(): pl.pallas_call(functools.partial(kernel, sizes), out_shape=jax.ShapeDtype...  47.1 us
    pallas_call x1, Pallas kernels, per_device(): pl.pallas_call(functools.partial(share, counts), out_shape=tuple((jax.Sha...  1.36 us

profile of v6, /device:TPU:1, one launch (start us, length us, event | category | flops | bytes accessed | tf_op | source)
XLA Modules:
  0.0 49.1 jit_solution(9617258072694370072)
XLA Ops:
  0.6 47.1 %sweep.1.out = f32[48,24]{1,0:T(8,128)} custom-call(f32[16,192,384]{2,1,0:T(8,128)} %contacts.1, f32[12,24]{1,0:T(8,128)} %bitcast.5, f32[12,24]{1,0:T(8,128)} %bitcast.6), custom_call_target="tpu_custom_call" | custom-call | tf_op jit(solution)/shard_map/sweep/pallas_call | solution.py:513
  47.7 1.4 %share.1 = (f32[16,24]{1,0:T(8,128)}, f32[12,24]{1,0:T(8,128)}, f32[12,24]{1,0:T(8,128)}) custom-call(f32[48,24]{1,0:T(8,128)} %sweep.1.out), custom_call_target="tpu_custom_call" | custom-call | tf_op jit(solution)/shard_map/share/pallas_call | solution.py:553

commit v7 on v5

--- a/solution.py
+++ b/solution.py
@@ -219,9 +219,9 @@
     def over(count, partner, both, action):
         def one(m, carry):
             device = partner(m)
-            action(device)
             if both:
                 action(across(device))
+            action(device)
             return carry
 
         lax.fori_loop(0, count - 1, one, 0)

time: 49.3 us -> 49.3 us (level)
  no operation moved by 1% of the time
where the time goes in v7:
time: 49.3 us; the launch traced here: 49.2 us
  Pallas kernels  48.6 us (99%)
  between operations  0.64 us (1%)
    pallas_call x1, Pallas kernels, per_device(): pl.pallas_call(functools.partial(kernel, sizes), out_shape=jax.ShapeDtype...  47.2 us
    pallas_call x1, Pallas kernels, per_device(): pl.pallas_call(functools.partial(share, counts), out_shape=tuple((jax.Sha...  1.36 us

profile of v7, /device:TPU:1, one launch (start us, length us, event | category | flops | bytes accessed | tf_op | source)
XLA Modules:
  0.0 49.2 jit_solution(10462043628219126495)
XLA Ops:
  0.6 47.2 %sweep.1.out = f32[48,24]{1,0:T(8,128)} custom-call(f32[16,192,384]{2,1,0:T(8,128)} %contacts.1, f32[12,24]{1,0:T(8,128)} %bitcast.5, f32[12,24]{1,0:T(8,128)} %bitcast.6), custom_call_target="tpu_custom_call" | custom-call | tf_op jit(solution)/shard_map/sweep/pallas_call | solution.py:515
  47.8 1.4 %share.1 = (f32[16,24]{1,0:T(8,128)}, f32[12,24]{1,0:T(8,128)}, f32[12,24]{1,0:T(8,128)}) custom-call(f32[48,24]{1,0:T(8,128)} %sweep.1.out), custom_call_target="tpu_custom_call" | custom-call | tf_op jit(solution)/shard_map/share/pallas_call | solution.py:555
